TPU v7x, 32 devices: a whole 2x2x4 slice. The times are simulated.
32 devices in a mesh: pole: 2 (over x), row: 8 (over z, y), col: 2 (over core).
Axes of the slice: x: 2, y: 2, z: 4, core: 2. Of those that a mesh axis runs over, the one named last changes fastest.
Arguments:
- ancestor_inverse: float32 [2, 24576, 12288], P(None, ('pole', 'row'), 'col'), parts along dimension 1, may hold values from -6 to 6
- factor_panels: float32 [4, 2, 24576, 128], P(None, None, ('pole', 'col', 'row')), parts along dimension 2, may hold values from -0.0546875 to 0.0546875
- diag_inverse: float32 [8, 2, 128, 128], P('pole'), parts along dimension 0, may hold values from -6 to 6
- coupling: float32 [4, 2, 128, 128], P('pole'), parts along dimension 0, may hold values from -0.5 to 0.5
- block_pattern: int32 [4, 96], replicated, may hold values from 0 to 1, as said below
- tree_order: int32 [4], replicated, may hold values from 0 to 3, each once
Outputs:
- inverse_panels: float32 [4, 2, 24576, 128], P(None, None, ('pole', 'row')), parts along dimension 2
- inverse_diagonal: float32 [8, 2, 128, 128], P('pole'), parts along dimension 0
- inverse_coupling: float32 [4, 2, 128, 128], P('pole'), parts along dimension 0
There are 2 independent parts, one for each index of `pole`. A program takes and returns all parts, laid end to end along the dimension named above; an argument that names none is the same for every part. Nothing has to cross between parts.
Inputs may be any that keep to these rules, and one draw needn't show every extreme that they name: `tree_order`: each supernode number appears once. `block_pattern`: blocks 0 and 48 lie in every supernode's structure.
All inputs are finite; a program needn't handle non-finite values.
Results may differ from a plain program's by a relative error of at most 0.0001.
Values sent between devices are 32-bit elements; how exact they have to be, the bound alone decides.
No kernel may reach another device: no remote copies, remote signals or barrier semaphores. Data moves between devices by JAX's collectives and lax.ppermute only.
A program may use at most 192 MiB of HBM per device.

v0:
```python
import jax
import jax.numpy as jnp
from jax import lax
from jax.sharding import PartitionSpec as P


def swapped(block, axis, bit):
    count = lax.axis_size(axis)
    route = []
    for low in range(count):
        high = low | 1 << bit
        if high != low and high < count:
            route += [(low, high), (high, low)]
    return lax.ppermute(block, axis, route)


def matmul(left_side, right_side):
    return jnp.dot(
        left_side, right_side, preferred_element_type=jnp.float32, precision=lax.Precision.HIGHEST
    )


def multiply(left_side, right_side):
    real_part = matmul(left_side[0], right_side[0]) - matmul(left_side[1], right_side[1])
    imag_part = matmul(left_side[0], right_side[1]) + matmul(left_side[1], right_side[0])
    return jnp.stack([real_part, imag_part])


def flipped(matrix):
    return jnp.swapaxes(matrix, 1, 2)


def row_masks(pattern_eff, first_row, row_count, block_rows):
    row_index = first_row + jnp.arange(row_count, dtype=jnp.int32)
    blocks = row_index // block_rows
    onehot = (blocks[:, None] == jnp.arange(pattern_eff.shape[1], dtype=jnp.int32)[None, :]).astype(
        jnp.float32
    )
    return matmul(pattern_eff, onehot.T)


def per_device(ancestor_inverse, factor_panels, diag_inverse, coupling, block_pattern, tree_order):
    grid_row = lax.axis_index("row")
    grid_col = lax.axis_index("col")
    tile_rows = ancestor_inverse.shape[1]
    half_rows = ancestor_inverse.shape[2]
    piece_rows = factor_panels.shape[2]
    block_rows = factor_panels.shape[3]
    super_count = factor_panels.shape[0]
    share_rows = tile_rows // 2
    sorted_pattern = jnp.take(block_pattern, tree_order, axis=0).astype(jnp.float32)
    pattern_eff = jnp.concatenate(
        [sorted_pattern[:2], sorted_pattern[2:] * sorted_pattern[:2]], axis=0
    )
    source_mask = row_masks(
        pattern_eff, grid_col * half_rows + grid_row * piece_rows, piece_rows, block_rows
    )
    target_mask = row_masks(pattern_eff, grid_row * tile_rows, tile_rows, block_rows)
    panels = jnp.take(factor_panels, tree_order, axis=0) * source_mask[:, None, :, None]
    diag_blocks = jnp.take(diag_inverse, tree_order, axis=0)
    columns = []
    products = []
    for tree_slot in range(super_count):
        gathered = lax.all_gather(panels[tree_slot], "row", axis=1, tiled=True)
        columns.append(gathered)
        products.append(lax.psum(multiply(ancestor_inverse, gathered), "col"))
    own_flag = (grid_row * tile_rows // half_rows == grid_col).astype(jnp.float32)
    offset = jnp.clip(grid_row * tile_rows - grid_col * half_rows, 0, half_rows - tile_rows)
    own_windows = jnp.stack(
        [
            lax.dynamic_slice_in_dim(column_set, offset, tile_rows, 1) * own_flag
            for column_set in columns
        ]
    )
    partner_windows = swapped(own_windows, "col", 0)
    tile_windows = own_windows + partner_windows

    def share(matrix):
        return lax.dynamic_slice_in_dim(matrix, grid_col * share_rows, share_rows, 1)

    windows = [share(tile_windows[tree_slot]) for tree_slot in range(super_count)]
    parent_cols = [
        -target_mask[tree_slot][None, :, None] * products[tree_slot] for tree_slot in range(2)
    ]
    child_cols = [
        -target_mask[tree_slot + 2][None, :, None]
        * (products[tree_slot + 2] + multiply(parent_cols[tree_slot], coupling[tree_slot]))
        for tree_slot in range(2)
    ]
    parent_local = [
        multiply(flipped(windows[tree_slot]), share(parent_cols[tree_slot]))
        for tree_slot in range(2)
    ]
    cross_local = [
        multiply(flipped(share(parent_cols[tree_slot])), windows[tree_slot + 2])
        for tree_slot in range(2)
    ]
    child_local = [
        multiply(flipped(windows[tree_slot + 2]), share(child_cols[tree_slot]))
        for tree_slot in range(2)
    ]
    parent_sums = lax.psum(jnp.stack(parent_local), ("row", "col"))
    parent_diag = [diag_blocks[tree_slot] - parent_sums[tree_slot] for tree_slot in range(2)]
    child_totals = lax.psum(jnp.stack(cross_local + child_local), ("row", "col"))
    crosses = [
        -(child_totals[tree_slot] + multiply(parent_diag[tree_slot], coupling[tree_slot]))
        for tree_slot in range(2)
    ]
    child_sums = [child_totals[2 + tree_slot] for tree_slot in range(2)]
    child_diag = [
        diag_blocks[tree_slot + 2]
        - child_sums[tree_slot]
        - multiply(flipped(coupling[tree_slot]), crosses[tree_slot])
        for tree_slot in range(2)
    ]
    all_cols = jnp.stack(parent_cols + child_cols)
    all_diag = jnp.stack(parent_diag + child_diag)
    inverse_panels = jnp.zeros_like(all_cols).at[tree_order].set(all_cols)
    inverse_diagonal = jnp.zeros_like(all_diag).at[tree_order].set(all_diag)
    return (inverse_panels, inverse_diagonal, jnp.stack(crosses))


def solution(mesh):
    return jax.shard_map(
        per_device,
        mesh=mesh,
        in_specs=(
            P(None, ("pole", "row"), "col"),
            P(None, None, ("pole", "col", "row"), None),
            P("pole", None, None, None),
            P("pole", None, None, None),
            P(),
            P(),
        ),
        out_specs=(
            P(None, None, ("pole", "row"), None),
            P("pole", None, None, None),
            P("pole", None, None, None),
        ),
        check_vma=False,
    )
```

profile of v0, /device:TPU:0, one launch (start us, length us, event | category | flops | bytes accessed | tf_op | source)
XLA Modules:
  0.0 877.5 jit_solution(7536772676169645142)
XLA Ops:
  19.7 99.8 %all-gather.11.cloned.1.call-done = f32[1,2,6144,128]{3,2,1,0:T(8,128)} async-done(((f32[1,2,768,128]{3,2,1,0:T(8,128)}), f32[1,2,6144,128]{3,2,1,0:T(8,128)}) %all-gather.11.cloned.1.call-update) | async-done | bytes 6291472 | tf_op jit(solution)/shard_map/all_gather | solution.py:64
  119.5 36.1 %fusion.8 = f32[128,1536]{1,0:T(8,128)S(1)} fusion(f32[2,1536,6144]{2,1,0:T(8,128)} %param.6, f32[1,2,6144,128]{3,2,1,0:T(8,128)} %all-gather.11.cloned.1.call-done), kind=kOutput, calls=%fused_computation.13 | convolution fusion | flops 14495514624 | bytes 41680896 | tf_op jit(solution)/shard_map/dot_general | solution.py:18
  155.6 35.0 %fusion.10 = f32[128,1536]{1,0:T(8,128)S(1)} fusion(f32[2,1536,6144]{2,1,0:T(8,128)} %param.6, f32[1,2,6144,128]{3,2,1,0:T(8,128)S(1)} %copy-done.2), kind=kOutput, calls=%fused_computation.15 | convolution fusion | flops 14495514624 | bytes 41680896 | tf_op jit(solution)/shard_map/dot_general | solution.py:18
  190.6 35.3 %fusion.73 = f32[1,1536,128]{1,2,0:T(8,128)S(1)} fusion(f32[128,1536]{1,0:T(8,128)S(1)} %fusion.8, f32[2,1536,6144]{2,1,0:T(8,128)} %param.6, f32[1,2,6144,128]{3,2,1,0:T(8,128)S(1)} %copy-done.2), kind=kOutput, calls=%fused_computation.79 | convolution fusion | flops 14495711232 | bytes 42467328 | tf_op jit(solution)/shard_map/dot_general | solution.py:18
  225.9 35.5 %fusion.67 = f32[1,1536,128]{1,2,0:T(8,128)S(1)} fusion(f32[128,1536]{1,0:T(8,128)S(1)} %fusion.10, f32[2,1536,6144]{2,1,0:T(8,128)} %param.6, f32[1,2,6144,128]{3,2,1,0:T(8,128)S(1)} %copy-done.2), kind=kOutput, calls=%fused_computation.77 | convolution fusion | flops 14495711232 | bytes 42467328 | tf_op jit(solution)/shard_map/dot_general | solution.py:18
  261.5 36.6 %fusion.4 = f32[128,1536]{1,0:T(8,128)S(1)} fusion(f32[2,1536,6144]{2,1,0:T(8,128)} %param.6, f32[1,2,6144,128]{3,2,1,0:T(8,128)} %all-gather.13.cloned.1.call-done), kind=kOutput, calls=%fused_computation.9 | convolution fusion | flops 14495514624 | bytes 41680896 | tf_op jit(solution)/shard_map/dot_general | solution.py:18
  298.1 35.3 %fusion.6 = f32[128,1536]{1,0:T(8,128)S(1)} fusion(f32[2,1536,6144]{2,1,0:T(8,128)} %param.6, f32[1,2,6144,128]{3,2,1,0:T(8,128)S(1)} %copy-done.3), kind=kOutput, calls=%fused_computation.11 | convolution fusion | flops 14495514624 | bytes 41680896 | tf_op jit(solution)/shard_map/dot_general | solution.py:18
  334.7 35.2 %fusion.85 = f32[1,1536,128]{1,2,0:T(8,128)S(1)} fusion(f32[128,1536]{1,0:T(8,128)S(1)} %fusion.4, f32[2,1536,6144]{2,1,0:T(8,128)} %param.6, f32[1,2,6144,128]{3,2,1,0:T(8,128)S(1)} %copy-done.3), kind=kOutput, calls=%fused_computation.83 | convolution fusion | flops 14495711232 | bytes 42467328 | tf_op jit(solution)/shard_map/dot_general | solution.py:18
  370.0 35.1 %fusion.79 = f32[1,1536,128]{1,2,0:T(8,128)S(1)} fusion(f32[128,1536]{1,0:T(8,128)S(1)} %fusion.6, f32[2,1536,6144]{2,1,0:T(8,128)} %param.6, f32[1,2,6144,128]{3,2,1,0:T(8,128)S(1)} %copy-done.3), kind=kOutput, calls=%fused_computation.81 | convolution fusion | flops 14495711232 | bytes 42467328 | tf_op jit(solution)/shard_map/dot_general | solution.py:18
  406.3 36.3 %fusion = f32[128,1536]{1,0:T(8,128)S(1)} fusion(f32[2,1536,6144]{2,1,0:T(8,128)} %param.6, f32[1,2,6144,128]{3,2,1,0:T(8,128)} %all-gather.15.cloned.1.call-done), kind=kOutput, calls=%fused_computation.5 | convolution fusion | flops 14495514624 | bytes 41680896 | tf_op jit(solution)/shard_map/dot_general | solution.py:18
  442.6 35.0 %fusion.2 = f32[128,1536]{1,0:T(8,128)S(1)} fusion(f32[2,1536,6144]{2,1,0:T(8,128)} %param.6, f32[1,2,6144,128]{3,2,1,0:T(8,128)S(1)} %copy-done.4), kind=kOutput, calls=%fused_computation.7 | convolution fusion | flops 14495514624 | bytes 41680896 | tf_op jit(solution)/shard_map/dot_general | solution.py:18
  477.7 35.5 %fusion.97 = f32[1,1536,128]{1,2,0:T(8,128)S(1)} fusion(f32[128,1536]{1,0:T(8,128)S(1)} %fusion, f32[2,1536,6144]{2,1,0:T(8,128)} %param.6, f32[1,2,6144,128]{3,2,1,0:T(8,128)S(1)} %copy-done.4), kind=kOutput, calls=%fused_computation.87 | convolution fusion | flops 14495711232 | bytes 42467328 | tf_op jit(solution)/shard_map/dot_general | solution.py:18
  513.2 35.0 %fusion.91 = f32[1,1536,128]{1,2,0:T(8,128)S(1)} fusion(f32[128,1536]{1,0:T(8,128)S(1)} %fusion.2, f32[2,1536,6144]{2,1,0:T(8,128)} %param.6, f32[1,2,6144,128]{3,2,1,0:T(8,128)S(1)} %copy-done.4), kind=kOutput, calls=%fused_computation.85 | convolution fusion | flops 14495711232 | bytes 42467328 | tf_op jit(solution)/shard_map/dot_general | solution.py:18
  549.5 36.3 %fusion.12 = f32[128,1536]{1,0:T(8,128)S(1)} fusion(f32[2,1536,6144]{2,1,0:T(8,128)} %param.6, f32[1,2,6144,128]{3,2,1,0:T(8,128)} %all-gather.9.cloned.1.call-done), kind=kOutput, calls=%fused_computation.17 | convolution fusion | flops 14495514624 | bytes 41680896 | tf_op jit(solution)/shard_map/dot_general | solution.py:18
  585.8 35.0 %fusion.14 = f32[128,1536]{1,0:T(8,128)S(1)} fusion(f32[2,1536,6144]{2,1,0:T(8,128)} %param.6, f32[1,2,6144,128]{3,2,1,0:T(8,128)S(1)} %copy-done.5), kind=kOutput, calls=%fused_computation.19 | convolution fusion | flops 14495514624 | bytes 41680896 | tf_op jit(solution)/shard_map/dot_general | solution.py:18
  620.8 35.5 %fusion.61 = f32[1,1536,128]{1,2,0:T(8,128)S(1)} fusion(f32[128,1536]{1,0:T(8,128)S(1)} %fusion.12, f32[2,1536,6144]{2,1,0:T(8,128)} %param.6, f32[1,2,6144,128]{3,2,1,0:T(8,128)S(1)} %copy-done.5), kind=kOutput, calls=%fused_computation.75 | convolution fusion | flops 14495711232 | bytes 42467328 | tf_op jit(solution)/shard_map/dot_general | solution.py:18
  656.3 35.0 %fusion.55 = f32[1,1536,128]{1,2,0:T(8,128)S(1)} fusion(f32[128,1536]{1,0:T(8,128)S(1)} %fusion.14, f32[2,1536,6144]{2,1,0:T(8,128)} %param.6, f32[1,2,6144,128]{3,2,1,0:T(8,128)S(1)} %copy-done.5), kind=kOutput, calls=%fused_computation.73 | convolution fusion | flops 14495711232 | bytes 42467328 | tf_op jit(solution)/shard_map/dot_general | solution.py:18
  709.9 17.7 %all-reduce.7.cloned.1.call-done = (f32[2,1536,128]{1,2,0:T(8,128)}, f32[2,1536,128]{1,2,0:T(8,128)}, f32[2,1536,128]{1,2,0:T(8,128)}, f32[2,1536,128]{1,2,0:T(8,128)}) async-done(((f32[2,1536,128]{1,2,0:T(8,128)}, f32[2,1536,128]{1,2,0:T(8,128)}, f32[2,1536,128]{1,2,0:T(8,128)}, f32[2,1536,128]{1,2,0:T(8,128)}), (f32[2,1536,128]{1,2,0:T(8,128)}, f32[2,1536,128]{1,2,0:T(8,128)}, f32[2,1536,128]{1,2,0:T(8,128)}, ...) | async-done | bytes 6291472 | tf_op jit(solution)/shard_map/psum | solution.py:66
  737.1 3.3 fusion.220
  765.3 4.3 pad_maximum_fusion
  769.6 6.6 copy.33
  776.2 3.2 broadcast_in_dim.45
  779.4 13.3 %scatter_fusion = f32[4,2,1536,128]{3,2,1,0:T(8,128)} fusion(f32[4,2,1536,128]{3,2,1,0:T(8,128)} %broadcast_in_dim.45, s32[4]{0:T(128)S(1)} %copy-done.32, f32[4,2,1536,128]{3,2,1,0:T(8,128)} %copy.33), kind=kCustom, calls=%fused_computation.3 | custom fusion | bytes 18874384 | tf_op jit(solution)/shard_map/scatter | solution.py:118
  792.7 66.1 %all-reduce.5.cloned.1.call-done = (f32[4,2,128,128]{3,2,1,0:T(8,128)}, f32[2,2,128,128]{3,2,1,0:T(8,128)}) async-done(((f32[4,2,128,128]{3,2,1,0:T(8,128)}, f32[2,2,128,128]{3,2,1,0:T(8,128)}), (f32[4,2,128,128]{3,2,1,0:T(8,128)}, f32[2,2,128,128]{3,2,1,0:T(8,128)})) %all-reduce.5.cloned.1.call-update) | async-done | bytes 786448 | tf_op jit(solution)/shard_map/psum | solution.py:104
  (191 shorter events, 79.8 us)
Async XLA Ops:
  7.2 112.3 %all-gather.11.cloned.1.call-start = ((), (), s32[]{:S(2)}) async-start(), calls=%async_computation.1 | async-start | bytes 7077888 | tf_op jit(solution)/shard_map/all_gather | solution.py:64
  8.0 5.4 copy-start.33
  17.6 243.9 %all-gather.13.cloned.1.call-start = ((), (), s32[]{:S(2)}) async-start(), calls=%async_computation.2 | async-start | bytes 7077888 | tf_op jit(solution)/shard_map/all_gather | solution.py:64
  18.3 387.9 %all-gather.15.cloned.1.call-start = ((), (), s32[]{:S(2)}) async-start(), calls=%async_computation.3 | async-start | bytes 7077888 | tf_op jit(solution)/shard_map/all_gather | solution.py:64
  19.1 530.4 %all-gather.9.cloned.1.call-start = ((), (), s32[]{:S(2)}) async-start(), calls=%async_computation | async-start | bytes 7077888 | tf_op jit(solution)/shard_map/all_gather | solution.py:64
  19.7 707.9 %all-reduce.7.cloned.1.call-start = ((), (), s32[]{:S(2)}) async-start(), calls=%async_computation.5 | async-start | bytes 12582912 | tf_op jit(solution)/shard_map/psum | solution.py:66
  119.5 36.1 %copy-start.2 = (f32[1,2,6144,128]{3,2,1,0:T(8,128)S(1)}, f32[1,2,6144,128]{3,2,1,0:T(8,128)}, u32[]{:S(2)}) copy-start(f32[1,2,6144,128]{3,2,1,0:T(8,128)} %all-gather.11.cloned.1.call-done) | copy-start | bytes 18874372
  261.5 36.6 %copy-start.3 = (f32[1,2,6144,128]{3,2,1,0:T(8,128)S(1)}, f32[1,2,6144,128]{3,2,1,0:T(8,128)}, u32[]{:S(2)}) copy-start(f32[1,2,6144,128]{3,2,1,0:T(8,128)} %all-gather.13.cloned.1.call-done) | copy-start | bytes 18874372
  406.3 36.3 %copy-start.4 = (f32[1,2,6144,128]{3,2,1,0:T(8,128)S(1)}, f32[1,2,6144,128]{3,2,1,0:T(8,128)}, u32[]{:S(2)}) copy-start(f32[1,2,6144,128]{3,2,1,0:T(8,128)} %all-gather.15.cloned.1.call-done) | copy-start | bytes 18874372
  549.5 36.3 %copy-start.5 = (f32[1,2,6144,128]{3,2,1,0:T(8,128)S(1)}, f32[1,2,6144,128]{3,2,1,0:T(8,128)}, u32[]{:S(2)}) copy-start(f32[1,2,6144,128]{3,2,1,0:T(8,128)} %all-gather.9.cloned.1.call-done) | copy-start | bytes 18874372
  692.7 166.1 %all-reduce.5.cloned.1.call-start = ((), (), s32[]{:S(2)}) async-start(), calls=%async_computation.4 | async-start | bytes 1572864 | tf_op jit(solution)/shard_map/psum | solution.py:104
  694.4 6.9 copy-start.10
  698.8 5.5 copy-start.14
  701.3 5.1 copy-start.35
  701.3 5.1 copy-start.37
  701.3 6.3 copy-start.18
  704.6 31.4 %collective-permute-start = (f32[4,2,1536,128]{3,2,1,0:T(8,128)}, f32[4,2,1536,128]{3,2,1,0:T(8,128)}, u32[]{:S(2)}, u32[]{:S(2)}) collective-permute-start(f32[4,2,1536,128]{3,2,1,0:T(8,128)} %pad_maximum_fusion.1), channel_id=1, source_target_pairs={{0,1},{1,0},{2,3},{3,2},{4,5},{5,4},{6,7},{7,6},{8,9},{9,8},{10,11... | collective-permute-start | bytes 18874376 | tf_op jit(solution)/shard_map/ppermute | solution.py:14
  750.6 9.5 %copy-start.8 = (f32[2,1536,128]{1,2,0:T(8,128)}, f32[2,1536,128]{1,2,0:T(8,128)S(1)}, u32[]{:S(2)}) copy-start(f32[2,1536,128]{1,2,0:T(8,128)S(1)} %get-tuple-element.36) | copy-start | bytes 4718596
  750.6 11.1 %copy-start.6 = (f32[2,1536,128]{1,2,0:T(8,128)}, f32[2,1536,128]{1,2,0:T(8,128)S(1)}, u32[]{:S(2)}) copy-start(f32[2,1536,128]{1,2,0:T(8,128)S(1)} %get-tuple-element.35) | copy-start | bytes 4718596
  779.4 79.4 %copy-start.21 = (f32[4,2,128,128]{3,2,1,0:T(8,128)S(1)}, f32[4,2,128,128]{3,2,1,0:T(8,128)}, u32[]{:S(2)}) copy-start(f32[4,2,128,128]{3,2,1,0:T(8,128)} %broadcast_select_fusion) | copy-start | bytes 1572868
  792.7 69.9 %copy-start.26 = (f32[2,128,128]{1,2,0:T(8,128)S(1)}, f32[2,128,128]{1,2,0:T(8,128)}, u32[]{:S(2)}) copy-start(f32[2,128,128]{1,2,0:T(8,128)} %get-tuple-element.31) | copy-start | bytes 393220
  858.8 6.2 copy-start.22
  858.8 6.2 copy-start.25
  863.8 6.4 copy-start.1
  (21 other events, 60.7 us)
Sparse Core Ops, SparseCore 0:
  17.7 101.7 all-gather.10
  121.7 97.1 all-gather.12
  221.1 97.1 all-gather.14
  321.0 97.2 all-gather.8
  692.8 34.7 all-reduce.6
  765.4 93.3 all-reduce.4
where the time goes:
time: 887 us; the launch traced here: 877 us
  matrix products  597 us (67%)
  waiting for transfers between devices  186 us (21%)
  other arithmetic  41.1 us (5%)
  local copies, waits for them, and re-layouts  38.2 us (4%)
  between operations  15.6 us (2%)
    dot_general x66, matrix products, matmul(): jnp.dot(left_side, right_side, preferred_element_type=jnp.float32, precis...  597 us
    all_gather x4, waiting for transfers between devices, per_device(): gathered = lax.all_gather(panels[tree_slot], 'row', axis=1, tiled=True)  99.8 us
    psum x1, waiting for transfers between devices, per_device(): lax.psum(jnp.stack(cross_local + child_local), ('row', 'col'))  66.1 us
  transfers between devices with their start and end apart: 7, of which 3 were waited for; matrix products, arithmetic and copies ran while one was open for 55% of the time, Pallas kernels for 0%

commit v1 on v0

--- a/solution.py
+++ b/solution.py
@@ -1,7 +1,567 @@
+import functools
+
 import jax
 import jax.numpy as jnp
 from jax import lax
+from jax.experimental import pallas as pl
+from jax.experimental.pallas import tpu as pltpu
 from jax.sharding import PartitionSpec as P
+
+
+def matmul(left_side, right_side):
+    return jnp.dot(
+        left_side, right_side, preferred_element_type=jnp.float32, precision=lax.Precision.HIGHEST
+    )
+
+
+def multiply(left_side, right_side):
+    real_part = matmul(left_side[0], right_side[0]) - matmul(left_side[1], right_side[1])
+    imag_part = matmul(left_side[0], right_side[1]) + matmul(left_side[1], right_side[0])
+    return jnp.stack([real_part, imag_part])
+
+
+def flipped(matrix):
+    return jnp.swapaxes(matrix, 1, 2)
+
+
+def halves(value):
+    high = value.astype(jnp.bfloat16)
+    low = (value - high.astype(jnp.float32)).astype(jnp.bfloat16)
+    return high, low
+
+
+def dot32(left_side, right_side, contract=((1,), (0,))):
+    return lax.dot_general(
+        left_side, right_side, (contract, ((), ())), preferred_element_type=jnp.float32
+    )
+
+
+def dot3(left_side, right_side, contract=((1,), (0,))):
+    return (
+        dot32(left_side[0], right_side[0], contract)
+        + dot32(left_side[0], right_side[1], contract)
+        + dot32(left_side[1], right_side[0], contract)
+    )
+
+
+ARRIVALS = (
+    ("own", False, (0, 1, 2, 3)),
+    ("right 1", False, (None, 0, 1, 2)),
+    ("left 1", False, (1, 2, 3, None)),
+    ("over 1", True, (0, 1, 2, 3)),
+    ("right 2", (False, True, False, False), (None, 0, 0, 1)),
+    ("left 2", (False, False, True, False), (2, 3, 3, None)),
+    ("over 2", True, (1, 2, 1, 2)),
+    ("right 3", False, (None, None, None, 0)),
+    ("left 3", False, (3, None, None, None)),
+    ("over 3", True, (2, 3, 0, 1)),
+    ("over 4", True, (3, None, None, 0)),
+)
+LINES = len(ARRIVALS[0][2])
+
+
+class Layout:
+    def __init__(self, rows, cols, a_shape, p_shape):
+        self.rows, self.cols = rows, cols
+        self.lines = rows // 2
+        self.slots, _, self.piece_rows, self.block = p_shape
+        self.tile_rows, self.half_rows = a_shape[1:]
+        self.piece_blocks = self.piece_rows // self.block
+        self.tile_blocks = self.tile_rows // self.block
+        self.half_blocks = self.half_rows // self.block
+        self.units = self.piece_blocks * self.slots
+        self.buffers = len(ARRIVALS)
+        self.group = next(size for size in (4, 3, 2, 1) if self.tile_blocks % size == 0)
+        self.ranks = 0
+        self.source = cols * rows * self.units
+        self.order = self.source + self.units
+        self.live = self.order + self.slots * self.tile_blocks
+        self.owners = self.live + self.slots
+        self.windows = self.owners + self.buffers
+        self.most = self.windows + 2
+        self.total = self.most + 1
+
+
+def plan_kernel(layout, place, pattern, order, plan):
+    row, col = place[0], place[1]
+    trees = layout.slots // 2
+    names = [order[slot] for slot in range(layout.slots)]
+
+    def live(slot, block):
+        value = pattern[names[slot], block]
+        if slot >= trees:
+            value = value * pattern[names[slot - trees], block]
+        return value
+
+    def of_owner(owner, most):
+        count = jnp.int32(0)
+        for piece in range(layout.piece_blocks):
+            for slot in range(layout.slots):
+                value = live(slot, owner * layout.piece_blocks + piece)
+                at = owner * layout.units + piece * layout.slots + slot
+                plan[layout.ranks + at] = jnp.where(value > 0, count, -1)
+                count = count + value
+        return jnp.maximum(most, count)
+
+    plan[layout.most] = lax.fori_loop(0, layout.cols * layout.rows, of_owner, jnp.int32(0))
+    for unit in range(layout.units):
+        plan[layout.source + unit] = 0
+    mine = (col * layout.rows + row) * layout.units
+    for unit in range(layout.units):
+        rank = plan[layout.ranks + mine + unit]
+
+        @pl.when(rank >= 0)
+        def _():
+            plan[layout.source + rank] = unit
+
+    for slot in range(layout.slots):
+        count = jnp.int32(0)
+        values = []
+        for index in range(layout.tile_blocks):
+            value = live(slot, row * layout.tile_blocks + index)
+            values.append(value)
+            count = count + value
+        plan[layout.live + slot] = count
+        front, back = jnp.int32(0), count
+        for index, value in enumerate(values):
+            at = layout.order + slot * layout.tile_blocks + jnp.where(value > 0, front, back)
+            plan[at] = index
+            front, back = front + value, back + 1 - value
+
+    line, side = row // 2, row % 2
+    window_line = (row * layout.tile_blocks % layout.half_blocks) // layout.piece_blocks // 2
+    windows = [jnp.int32(0), jnp.int32(0)]
+    for index, (_, across, origins) in enumerate(ARRIVALS):
+        owner = jnp.int32(-1)
+        for at, origin in enumerate(origins):
+            if origin is not None:
+                crossed = across if isinstance(across, bool) else across[at]
+                from_side = 1 - side if crossed else side
+                owner = jnp.where(line == at, origin * 2 + from_side, owner)
+        plan[layout.owners + index] = owner
+        for which in range(2):
+            hit = owner == window_line * 2 + which
+            windows[which] = jnp.where(hit, index, windows[which])
+    for which in range(2):
+        plan[layout.windows + which] = windows[which]
+
+
+def make_plan(layout, row, col, block_pattern, tree_order):
+    smem = pl.BlockSpec(memory_space=pltpu.SMEM)
+    return pl.pallas_call(
+        functools.partial(plan_kernel, layout),
+        out_shape=jax.ShapeDtypeStruct((layout.total,), jnp.int32),
+        in_specs=[smem] * 3,
+        out_specs=smem,
+        name="make_plan",
+    )(jnp.stack([row, col]).astype(jnp.int32), block_pattern, tree_order)
+
+
+def compact_kernel(layout, plan, order, panels, units, sems):
+    block = layout.block
+    copies = []
+    for unit in range(units.shape[0]):
+        source = plan[layout.source + unit]
+        first = pl.multiple_of(source // layout.slots * block, block)
+        copy = pltpu.make_async_copy(
+            panels.at[order[source % layout.slots], :, pl.ds(first, block), :],
+            units.at[unit],
+            sems.at[unit],
+        )
+        copy.start()
+        copies.append(copy)
+    for copy in copies:
+        copy.wait()
+
+
+def compact_units(layout, plan, tree_order, panels):
+    shape = (layout.units, 2, layout.block, layout.block)
+    return pl.pallas_call(
+        functools.partial(compact_kernel, layout),
+        out_shape=jax.ShapeDtypeStruct(shape, jnp.float32),
+        grid_spec=pltpu.PrefetchScalarGridSpec(
+            num_scalar_prefetch=2,
+            grid=(1,),
+            in_specs=[pl.BlockSpec(memory_space=pltpu.HBM)],
+            out_specs=pl.BlockSpec(shape, lambda step, plan, order: (0, 0, 0, 0)),
+            scratch_shapes=[pltpu.SemaphoreType.DMA((layout.units,))],
+        ),
+        compiler_params=pltpu.CompilerParams(vmem_limit_bytes=16 * 2**20),
+        name="compact_units",
+    )(plan, tree_order, panels)
+
+
+def owner_at(layout, which, plan, step):
+    owner = plan[layout.owners + which[0]]
+    for local in range(1, len(which)):
+        later = step // layout.piece_blocks >= local
+        owner = jnp.where(later, plan[layout.owners + which[local]], owner)
+    return owner
+
+
+def gemm_kernel(layout, which, first_call, plan, place, *refs):
+    refs = list(refs)
+    in_ref = None if first_call else refs.pop(0)
+    a_ref = refs.pop(0)
+    units = refs[: len(which)]
+    out_ref, total, a_parts, weights, sem = refs[len(which) :]
+    step = pl.program_id(0)
+    block, group = layout.block, layout.group
+    width = 2 * block
+    rows = layout.tile_rows
+    span_rows = group * block
+
+    @pl.when(step == 0)
+    def _():
+        if first_call:
+            total[...] = jnp.zeros_like(total)
+        else:
+            load = pltpu.make_async_copy(in_ref, total, sem)
+            load.start()
+            load.wait()
+
+    owner = owner_at(layout, which, plan, step)
+
+    @pl.loop(0, jnp.where(owner >= 0, rows // block, 0))
+    def _(index):
+        span = pl.ds(pl.multiple_of(index * block, block), block)
+        for part in range(2):
+            high, low = halves(a_ref[part, span, :])
+            a_parts[span, part * block : (part + 1) * block] = high
+            a_parts[span, width + part * block : width + (part + 1) * block] = low
+            a_parts[span, 2 * width + part * block : 2 * width + (part + 1) * block] = high
+
+    base = place[1] * layout.rows * layout.units + owner * layout.units
+    base = base + step % layout.piece_blocks * layout.slots
+
+    @pl.loop(0, jnp.where(owner >= 0, layout.slots, 0))
+    def _(slot):
+        rank = plan[layout.ranks + base + slot]
+
+        for local in range(len(which)):
+
+            @pl.when((rank >= 0) & (step // layout.piece_blocks == local))
+            def _():
+                real, imag = units[local][rank, 0], units[local][rank, 1]
+                real_parts, imag_parts = halves(real), halves(imag)
+                for third, part in enumerate((0, 0, 1)):
+                    top = third * width
+                    weights[top : top + block, :block] = real_parts[part]
+                    weights[top : top + block, block:] = imag_parts[part]
+                    weights[top + block : top + width, :block] = -imag_parts[part]
+                    weights[top + block : top + width, block:] = real_parts[part]
+
+        count = plan[layout.live + slot]
+
+        @pl.loop(0, jnp.where(rank >= 0, (count + group - 1) // group, 0))
+        def _(index):
+            spans = []
+            for at in range(group):
+                first = plan[layout.order + slot * layout.tile_blocks + index * group + at]
+                spans.append(pl.ds(pl.multiple_of(first * block, block), block))
+            left_side = jnp.concatenate([a_parts[span, :] for span in spans], axis=0)
+            product = dot32(left_side, weights[...])
+            for at, span in enumerate(spans):
+                total[slot, span, :] += product[at * block : (at + 1) * block]
+
+    @pl.when(step == pl.num_programs(0) - 1)
+    def _():
+        store = pltpu.make_async_copy(total, out_ref, sem)
+        store.start()
+        store.wait()
+
+
+def gemm_units(layout, plan, place, total, ancestor_inverse, buffers, which):
+    first_call = total is None
+    totals = [] if first_call else [total]
+    hbm = pl.BlockSpec(memory_space=pltpu.HBM)
+    block, pieces = layout.block, layout.piece_blocks
+    rows, width = layout.tile_rows, 2 * layout.block
+
+    def column(step, plan, place):
+        owner = owner_at(layout, which, plan, step)
+        return 0, 0, jnp.where(owner >= 0, owner * pieces + step % pieces, 0)
+
+    shape = (layout.slots, rows, width)
+    steps = len(which) * pieces
+    return pl.pallas_call(
+        functools.partial(gemm_kernel, layout, which, first_call),
+        out_shape=jax.ShapeDtypeStruct(shape, jnp.float32),
+        grid_spec=pltpu.PrefetchScalarGridSpec(
+            num_scalar_prefetch=2,
+            grid=(steps,),
+            in_specs=[hbm] * len(totals)
+            + [pl.BlockSpec((2, rows, block), column)]
+            + [
+                pl.BlockSpec(
+                    buffer.shape,
+                    lambda step, plan, place: (0, 0, 0, 0),
+                    pipeline_mode=pl.Buffered(1),
+                )
+                for buffer in buffers
+            ],
+            out_specs=hbm,
+            scratch_shapes=[
+                pltpu.VMEM(shape, jnp.float32),
+                pltpu.VMEM((rows, 3 * width), jnp.bfloat16),
+                pltpu.VMEM((3 * width, width), jnp.bfloat16),
+                pltpu.SemaphoreType.DMA,
+            ],
+        ),
+        input_output_aliases={} if first_call else {2: 0},
+        compiler_params=pltpu.CompilerParams(vmem_limit_bytes=30 * 2**20),
+        cost_estimate=pl.CostEstimate(
+            flops=steps * layout.slots * 3 * 2 * rows * width * width // 2,
+            bytes_accessed=steps * rows * block * 8 + 8 * layout.slots * rows * width,
+            transcendentals=0,
+        ),
+        name="gemm_units",
+    )(plan, place, *totals, ancestor_inverse, *buffers)
+
+
+def finish_kernel(layout, step_blocks, plan, place, order, mine, other, coupling, *refs):
+    buffers = refs[: layout.buffers]
+    columns, sums, acc, held, sems = refs[layout.buffers :]
+    step = pl.program_id(0)
+    block, slots, trees = layout.block, layout.slots, layout.slots // 2
+    row, col = place[0], place[1]
+    holds = row * layout.tile_blocks // layout.half_blocks == col
+    inner = row * layout.tile_blocks % layout.half_blocks
+    base = col * layout.rows * layout.units + inner * slots
+
+    def fetch(which, index):
+        return pltpu.make_async_copy(buffers[index], held.at[which], sems.at[which])
+
+    @pl.when(step == 0)
+    def _():
+        acc[...] = jnp.zeros_like(acc)
+        for act in ("start", "wait"):
+            for which in range(2):
+                for index in range(layout.buffers):
+
+                    @pl.when(holds & (plan[layout.windows + which] == index))
+                    def _():
+                        getattr(fetch(which, index), act)()
+
+    def window(slot):
+        parts = []
+        for at in range(step_blocks):
+            index = step * step_blocks + at
+            rank = plan[layout.ranks + base + index * slots + slot]
+            which, place_in = index // layout.piece_blocks, jnp.maximum(rank, 0)
+            unit = held[which, place_in]
+            whole = jnp.concatenate([unit[0], unit[1]], axis=1)
+            parts.append(jnp.where(rank >= 0, whole, 0.0))
+        return halves(jnp.concatenate(parts, axis=0))
+
+    def masked(slot, value):
+        parts = []
+        for at in range(step_blocks):
+            alive = is_live(slot, step * step_blocks + at)
+            parts.append(jnp.where(alive, -value[at * block : (at + 1) * block], 0.0))
+        return jnp.concatenate(parts, axis=0)
+
+    def is_live(slot, index):
+        alive = jnp.bool_(False)
+        for at in range(layout.tile_blocks):
+            found = plan[layout.order + slot * layout.tile_blocks + at] == index
+            alive = alive | (found & (at < plan[layout.live + slot]))
+        return alive
+
+    def put(slot, value):
+        columns[order[slot], 0] = value[:, :block]
+        columns[order[slot], 1] = value[:, block:]
+
+    rows_first = ((0,), (0,))
+    for tree in range(trees):
+        child = tree + trees
+        real, imag = coupling[tree, 0], coupling[tree, 1]
+        link = jnp.concatenate(
+            [jnp.concatenate([real, imag], axis=1), jnp.concatenate([-imag, real], axis=1)], axis=0
+        )
+        parent_col = masked(tree, mine[tree] + other[tree])
+        put(tree, parent_col)
+        parent_parts = halves(parent_col)
+        linked = dot3(parent_parts, halves(link))
+        child_col = masked(child, mine[child] + other[child] + linked)
+        put(child, child_col)
+
+        @pl.when(holds)
+        def _():
+            child_panel = window(child)
+            acc[3 * tree] += dot3(window(tree), parent_parts, rows_first)
+            acc[3 * tree + 1] += dot3(child_panel, parent_parts, rows_first)
+            acc[3 * tree + 2] += dot3(child_panel, halves(child_col), rows_first)
+
+    @pl.when(step == pl.num_programs(0) - 1)
+    def _():
+        for index in range(3 * trees):
+            value = acc[index]
+            sums[index, 0] = value[:block, :block] - value[block:, block:]
+            sums[index, 1] = value[:block, block:] + value[block:, :block]
+
+
+def finish_columns(layout, plan, place, tree_order, mine, other, coupling, buffers):
+    block, slots = layout.block, layout.slots
+    rows, width = layout.tile_rows, 2 * layout.block
+    step_blocks = 2 if layout.piece_blocks % 2 == 0 else 1
+    step_rows = step_blocks * block
+    half = pl.BlockSpec((slots, step_rows, width), lambda step, *_: (0, step, 0))
+    sums_shape = (3 * slots // 2, 2, block, block)
+    return pl.pallas_call(
+        functools.partial(finish_kernel, layout, step_blocks),
+        out_shape=(
+            jax.ShapeDtypeStruct((slots, 2, rows, block), jnp.float32),
+            jax.ShapeDtypeStruct(sums_shape, jnp.float32),
+        ),
+        grid_spec=pltpu.PrefetchScalarGridSpec(
+            num_scalar_prefetch=3,
+            grid=(rows // step_rows,),
+            in_specs=[half, half, pl.BlockSpec(coupling.shape, lambda step, *_: (0, 0, 0, 0))]
+            + [pl.BlockSpec(memory_space=pl.ANY)] * layout.buffers,
+            out_specs=[
+                pl.BlockSpec((slots, 2, step_rows, block), lambda step, *_: (0, 0, step, 0)),
+                pl.BlockSpec(sums_shape, lambda step, *_: (0, 0, 0, 0)),
+            ],
+            scratch_shapes=[
+                pltpu.VMEM((3 * slots // 2, width, width), jnp.float32),
+                pltpu.VMEM((2,) + buffers[0].shape, jnp.float32),
+                pltpu.SemaphoreType.DMA((2,)),
+            ],
+        ),
+        compiler_params=pltpu.CompilerParams(vmem_limit_bytes=24 * 2**20),
+        name="finish_columns",
+    )(plan, place, tree_order, mine, other, coupling, *buffers)
+
+
+def complex_dot(left_side, right_side, contract=((1,), (0,))):
+    def dot(left_part, right_part):
+        return dot3(halves(left_side[left_part]), halves(right_side[right_part]), contract)
+
+    return dot(0, 0) - dot(1, 1), dot(0, 1) + dot(1, 0)
+
+
+def diagonal_kernel(order, sums, diag_in, coupling, diag_out, cross_out):
+    trees = coupling.shape[0]
+    for tree in range(trees):
+        parent, child = order[tree], order[tree + trees]
+        link = (coupling[tree, 0], coupling[tree, 1])
+        parent_diag = tuple(diag_in[parent, part] - sums[3 * tree, part] for part in range(2))
+        moved = complex_dot(parent_diag, link)
+        cross = tuple(-(sums[3 * tree + 1, part].T + moved[part]) for part in range(2))
+        back = complex_dot(link, cross, ((0,), (0,)))
+        for part in range(2):
+            diag_out[parent, part] = parent_diag[part]
+            cross_out[tree, part] = cross[part]
+            diag_out[child, part] = diag_in[child, part] - sums[3 * tree + 2, part] - back[part]
+
+
+def finish_diagonals(order, sums, diag_inverse, coupling):
+    vmem = pl.BlockSpec(memory_space=pltpu.VMEM)
+    return pl.pallas_call(
+        diagonal_kernel,
+        out_shape=(
+            jax.ShapeDtypeStruct(diag_inverse.shape, jnp.float32),
+            jax.ShapeDtypeStruct(coupling.shape, jnp.float32),
+        ),
+        in_specs=[pl.BlockSpec(memory_space=pltpu.SMEM), vmem, vmem, vmem],
+        out_specs=(vmem, vmem),
+        name="finish_diagonals",
+    )(order, sums, diag_inverse, coupling)
+
+
+def shift(value, stride):
+    count = lax.axis_size("row")
+    return lax.ppermute(
+        value, "row", [(at, at + stride) for at in range(count) if 0 <= at + stride < count]
+    )
+
+
+def swap(value, axis):
+    return lax.ppermute(value, axis, [(at, at ^ 1) for at in range(lax.axis_size(axis))])
+
+
+def pick(values, index):
+    return lax.dynamic_index_in_dim(values, index, 0, keepdims=False)
+
+
+def sum_devices(layout, sums, row, col):
+    lines, line, side = layout.lines, row // 2, row % 2
+    parts = sums.reshape(2, 2, lines, -1, layout.block)
+    mine = pick(parts, col) + swap(pick(parts, 1 - col), "col")
+    mine = pick(mine, side) + swap(pick(mine, 1 - side), "row")
+
+    def turn(value, by):
+        route = [
+            (2 * at + side, 2 * ((at + by) % lines) + side)
+            for at in range(lines)
+            for side in range(2)
+        ]
+        return lax.ppermute(value, "row", route)
+
+    came = [turn(pick(mine, (line + by) % lines), by) for by in range(1, lines)]
+    share = sum(came, pick(mine, line))
+    others = [share] + [turn(share, by) for by in range(1, lines)]
+    stacked = jnp.stack(others)
+    whole = jnp.zeros_like(stacked)
+    for by in range(lines):
+        whole = lax.dynamic_update_index_in_dim(whole, others[by], (line - by) % lines, 0)
+    far = swap(whole, "row")
+    sides = jnp.stack([jnp.where(side == 0, whole, far), jnp.where(side == 0, far, whole)])
+    beside = swap(sides, "col")
+    trees = jnp.stack([jnp.where(col == 0, sides, beside), jnp.where(col == 0, beside, sides)])
+    return trees.reshape(sums.shape)
+
+
+def live_units(ancestor_inverse, factor_panels, diag_inverse, coupling, block_pattern, tree_order):
+    layout = Layout(
+        lax.axis_size("row"), lax.axis_size("col"), ancestor_inverse.shape, factor_panels.shape
+    )
+    row, col = lax.axis_index("row"), lax.axis_index("col")
+    place = jnp.stack([row, col]).astype(jnp.int32)
+    line = row // 2
+    plan = make_plan(layout, row, col, block_pattern, tree_order)
+    units = compact_units(layout, plan, tree_order, factor_panels)
+
+    def gather_and_multiply(room, units):
+        own = lax.slice_in_dim(units, 0, room, axis=0)
+        arrived = {(0, 0): own}
+        half = room // 2
+
+        def multiplied(total, buffers, first):
+            which = list(range(first, first + len(buffers)))
+            return gemm_units(layout, plan, place, total, ancestor_inverse, buffers, which)
+
+        def phase(right, left, over, total, buffers, first):
+            came = shift(right, 2), shift(left, -2), swap(over, "row")
+            total = multiplied(total, buffers, first)
+            return lax.optimization_barrier((came, total))
+
+        def inward(values):
+            return jnp.where(line < LINES // 2, values[1], values[0])
+
+        first, total = phase(own, own, own, None, [own], 0)
+        right = jnp.where(line == 0, first[2], first[0])
+        left = jnp.where(line == LINES - 1, first[2], first[1])
+        second, total = phase(right, left, inward(first), total, list(first), 1)
+        third, total = phase(second[0], second[1], inward(second), total, list(second), 4)
+        rest = lax.slice_in_dim(third[2], room - half, room, axis=0)
+        over = lax.slice_in_dim(inward(third), 0, room - half, axis=0)
+        last, total = phase(rest, rest, over, total, list(third), 7)
+        fourth = jnp.concatenate([last[2], inward(last)])
+        total = multiplied(total, [fourth], 10)
+        buffers = [own, *first, *second, *third, fourth]
+        other = swap(total, "col")
+        return finish_columns(layout, plan, place, tree_order, total, other, coupling, buffers)
+
+    most = plan[layout.most]
+    rooms = sorted({-(-layout.units * part // 24) for part in (15, 16, 17, 18, 19, 20, 22, 24)})
+    choice = sum((most > room).astype(jnp.int32) for room in rooms[:-1])
+    branches = [functools.partial(gather_and_multiply, room) for room in rooms]
+    inverse_panels, sums = lax.switch(choice, branches, units)
+    sums = sum_devices(layout, sums, row, col)
+    inverse_diagonal, inverse_coupling = finish_diagonals(tree_order, sums, diag_inverse, coupling)
+    return inverse_panels, inverse_diagonal, inverse_coupling
 
 
 def swapped(block, axis, bit):
@@ -14,22 +574,6 @@
     return lax.ppermute(block, axis, route)
 
 
-def matmul(left_side, right_side):
-    return jnp.dot(
-        left_side, right_side, preferred_element_type=jnp.float32, precision=lax.Precision.HIGHEST
-    )
-
-
-def multiply(left_side, right_side):
-    real_part = matmul(left_side[0], right_side[0]) - matmul(left_side[1], right_side[1])
-    imag_part = matmul(left_side[0], right_side[1]) + matmul(left_side[1], right_side[0])
-    return jnp.stack([real_part, imag_part])
-
-
-def flipped(matrix):
-    return jnp.swapaxes(matrix, 1, 2)
-
-
 def row_masks(pattern_eff, first_row, row_count, block_rows):
     row_index = first_row + jnp.arange(row_count, dtype=jnp.int32)
     blocks = row_index // block_rows
@@ -39,7 +583,7 @@
     return matmul(pattern_eff, onehot.T)
 
 
-def per_device(ancestor_inverse, factor_panels, diag_inverse, coupling, block_pattern, tree_order):
+def whole_panels(ancestor_inverse, factor_panels, diag_inverse, coupling, block_pattern, tree_order):
     grid_row = lax.axis_index("row")
     grid_col = lax.axis_index("col")
     tile_rows = ancestor_inverse.shape[1]
@@ -120,6 +664,17 @@
     return (inverse_panels, inverse_diagonal, jnp.stack(crosses))
 
 
+def per_device(ancestor_inverse, factor_panels, *others):
+    row_count, col_count = lax.axis_size("row"), lax.axis_size("col")
+    piece_rows, block = factor_panels.shape[2:]
+    tile_rows, half_rows = ancestor_inverse.shape[1:]
+    whole_blocks = piece_rows % block == 0 and half_rows % tile_rows == 0
+    even_shares = row_count == 2 * LINES and 3 * block % LINES == 0
+    if whole_blocks and col_count == 2 and even_shares:
+        return live_units(ancestor_inverse, factor_panels, *others)
+    return whole_panels(ancestor_inverse, factor_panels, *others)
+
+
 def solution(mesh):
     return jax.shard_map(
         per_device,

time: 887 us -> 368 us (0.41)
  matrix products: 597 us -> 0 us
  Pallas kernels: 0 us -> 169 us
  waiting for transfers between devices: 186 us -> 106 us
  starting transfers between devices: 0.24 us -> 45.6 us
  other arithmetic: 41.1 us -> 6.73 us
  local copies, waits for them, and re-layouts: 38.2 us -> 9.9 us
  loops' own time: 0 us -> 17.9 us
  between operations: 15.6 us -> 5.84 us
    dot_general x66 -> x0, matrix products: 597 us -> none  [matmul(): jnp.dot(left_side, right_side, preferred_element_type=jnp.float32, precis...]
    pallas_call x0 -> x9, Pallas kernels: none -> 169 us  [the longest x5 143 us: gemm_units(): pl.pallas_call(functools.partial(gemm_kernel, layout, which, first_call),...]
    ppermute x1 -> x23, waiting for transfers between devices: 0.01 us -> 106 us  [the longest x8 64.1 us: shift(): lax.ppermute(value, 'row', [(at, at + stride) for at in range(count) if 0...]
    all_gather x4 -> x0, waiting for transfers between devices: 99.8 us -> none  [per_device(): gathered = lax.all_gather(panels[tree_slot], 'row', axis=1, tiled=True)]
    psum x2 -> x0, waiting for transfers between devices: 83.8 us -> none  [the longest x1 66.1 us: per_device(): lax.psum(jnp.stack(cross_local + child_local), ('row', 'col'))]
    ppermute x1 -> x23, starting transfers between devices: 0.01 us -> 45.6 us  [the longest x8 22.5 us: shift(): lax.ppermute(value, 'row', [(at, at + stride) for at in range(count) if 0...]
    another operation x0 -> x1, loops' own time: none -> 17.9 us  [live_units(): inverse_panels, sums = lax.switch(choice, branches, units)]
    another operation x18 -> x5, other arithmetic: 18.3 us -> 1.14 us  [the longest x2 1.01 us: sum_devices(): jnp.stack([jnp.where(col == 0, sides, beside), jnp.where(col == 0, beside...]
  transfers between devices with their start and end apart: 7 -> 23, of which waited for: 3 -> 18; matrix products, arithmetic and copies ran while one was open for 55% -> 0% of each run, Pallas kernels for 0% -> 35%
where the time goes in v1:
time: 368 us; the launch traced here: 361 us
  Pallas kernels  169 us (46%)
  waiting for transfers between devices  106 us (29%)
  starting transfers between devices  45.6 us (12%)
  loops' own time  17.9 us (5%)
  local copies, waits for them, and re-layouts  9.9 us (3%)
  other arithmetic  6.73 us (2%)
  between operations  5.84 us (2%)
    pallas_call x5, Pallas kernels, gemm_units(): pl.pallas_call(functools.partial(gemm_kernel, layout, which, first_call),...  143 us
    ppermute x8, waiting for transfers between devices, shift(): lax.ppermute(value, 'row', [(at, at + stride) for at in range(count) if 0...  64.1 us
    ppermute x9, waiting for transfers between devices, swap(): lax.ppermute(value, axis, [(at, at ^ 1) for at in range(lax.axis_size(axi...  34.6 us
    ppermute x8, starting transfers between devices, shift(): lax.ppermute(value, 'row', [(at, at + stride) for at in range(count) if 0...  22.5 us
    another operation x1, loops' own time, live_units(): inverse_panels, sums = lax.switch(choice, branches, units)  17.9 us
    pallas_call x1, Pallas kernels, finish_columns(): pl.pallas_call(functools.partial(finish_kernel, layout, step_blocks), out...  16.8 us
    ppermute x9, starting transfers between devices, swap(): lax.ppermute(value, axis, [(at, at ^ 1) for at in range(lax.axis_size(axi...  13.1 us
    ppermute x6, starting transfers between devices, turn(): return lax.ppermute(value, 'row', route)  10 us
  transfers between devices with their start and end apart: 23, of which 18 were waited for; matrix products, arithmetic and copies ran while one was open for 0% of the time, Pallas kernels for 35%

profile of v1, /device:TPU:0, one launch (start us, length us, event | category | flops | bytes accessed | tf_op | source)
XLA Modules:
  0.0 360.9 jit_solution(8982516114186500447)
XLA Ops:
  6.1 3.4 compact_units.1
  14.1 300.8 %conditional.1 = (f32[4,2,1536,128]{3,2,1,0:T(8,128)}, f32[2,2,4,96,128]{4,3,2,1,0:T(8,128)}) conditional(s32[]{:T(128)} %bitcast.10, (s32[]{:T(128)}, f32[24,2,128,128]{3,2,1,0:T(8,128)S(1)}, s32[474]{0:T(512)S(1)}, s32[2]{0:T(128)S(1)}, f32[2,1536,6144]{2,1,0:T(8,128)}, /*index=5*/s32[4]{0:T(128)S(1)}, ...), branch_computations={%region_0.1_spmd, %region_1.2_spmd, %region_2.3_spmd, %region_3.4_... | conditional | flops 79730049024 | bytes 597689152 | solution.py:561
  23.8 5.1 %collective-permute-start.65 = (f32[20,2,128,128]{3,2,1,0:T(8,128)}, f32[20,2,128,128]{3,2,1,0:T(8,128)S(1)}, u32[]{:S(2)}, u32[]{:S(2)}) collective-permute-start(f32[20,2,128,128]{3,2,1,0:T(8,128)} %slice.63.refs_1_.refs_0_), channel_id=1, source_target_pairs={{0,4},{2,6},{4,8},{6,10},{8,12},{10,14},{1,5},{3,7},{5,9},{7,11},{... | collective-permute-start | bytes 7864328 | tf_op jit(solution)/shard_map/cond/branch_5_fun/ppermute | solution.py:475
  32.0 18.6 %gemm_units.65.refs_0_ = f32[4,1536,256]{2,1,0:T(8,128)S(1)} custom-call(s32[474]{0:T(512)S(1)} %get-tuple-element.254.plan, s32[2]{0:T(128)S(1)} %get-tuple-element.255.place, f32[2,1536,6144]{2,1,0:T(8,128)} %get-tuple-element.259.refs_0_.refs_1_, f32[20,2,128,128]{3,2,1,0:T(8,128)} %slice.63.refs_1_.refs_0_), custom_call_target="tpu_custom_call" | custom-call | flops 7247757312 | bytes 22020096 | tf_op jit(solution)/shard_map/cond/branch_5_fun/gemm_units/pallas_call | solution.py:287
  50.5 34.6 %collective-permute-done.65.refs_2_.refs_1_ = f32[20,2,128,128]{3,2,1,0:T(8,128)S(1)} collective-permute-done((f32[20,2,128,128]{3,2,1,0:T(8,128)}, f32[20,2,128,128]{3,2,1,0:T(8,128)S(1)}, u32[]{:S(2)}, u32[]{:S(2)}) %collective-permute-start.65) | collective-permute-done | bytes 2621472 | tf_op jit(solution)/shard_map/cond/branch_5_fun/ppermute | solution.py:475
  85.1 4.3 %collective-permute-done.66.refs_3_.refs_2_ = f32[20,2,128,128]{3,2,1,0:T(8,128)} collective-permute-done((f32[20,2,128,128]{3,2,1,0:T(8,128)}, f32[20,2,128,128]{3,2,1,0:T(8,128)}, u32[]{:S(2)}, u32[]{:S(2)}) %collective-permute-start.66) | collective-permute-done | bytes 2621472 | tf_op jit(solution)/shard_map/cond/branch_5_fun/ppermute | solution.py:475
  89.4 3.6 broadcast_select_fusion.26
  93.0 4.1 %collective-permute-start.68 = (f32[20,2,128,128]{3,2,1,0:T(8,128)S(1)}, f32[20,2,128,128]{3,2,1,0:T(8,128)S(1)}, u32[]{:S(2)}, u32[]{:S(2)}) collective-permute-start(f32[20,2,128,128]{3,2,1,0:T(8,128)S(1)} %get-tuple-element.358), channel_id=1, source_target_pairs={{0,4},{2,6},{4,8},{6,10},{8,12},{10,14},{1,5},{3,7},{5,9},{7,11},{... | collective-permute-start | bytes 7864328 | tf_op jit(solution)/shard_map/cond/branch_5_fun/ppermute | solution.py:475
  100.0 38.4 %gemm_units.66.refs_0_ = f32[4,1536,256]{2,1,0:T(8,128)S(1)} custom-call(s32[474]{0:T(512)S(1)} %get-tuple-element.254.plan, s32[2]{0:T(128)S(1)} %get-tuple-element.255.place, f32[4,1536,256]{2,1,0:T(8,128)S(1)} %gemm_units.65.refs_0_, f32[2,1536,6144]{2,1,0:T(8,128)} %get-tuple-element.259.refs_0_.refs_1_, ...), custom_call_target="tpu_custom_call", output_to_operand_aliasing={{}: (2, {})} | custom-call | flops 21743271936 | bytes 40894464 | tf_op jit(solution)/shard_map/cond/branch_5_fun/gemm_units/pallas_call | solution.py:287
  138.3 13.2 %collective-permute-done.68.refs_2_.refs_4_ = f32[20,2,128,128]{3,2,1,0:T(8,128)S(1)} collective-permute-done((f32[20,2,128,128]{3,2,1,0:T(8,128)S(1)}, f32[20,2,128,128]{3,2,1,0:T(8,128)S(1)}, u32[]{:S(2)}, u32[]{:S(2)}) %collective-permute-start.68) | collective-permute-done | bytes 2621472 | tf_op jit(solution)/shard_map/cond/branch_5_fun/ppermute | solution.py:475
  151.5 4.3 %collective-permute-done.69.refs_3_.refs_5_ = f32[20,2,128,128]{3,2,1,0:T(8,128)S(1)} collective-permute-done((f32[20,2,128,128]{3,2,1,0:T(8,128)S(1)}, f32[20,2,128,128]{3,2,1,0:T(8,128)S(1)}, u32[]{:S(2)}, u32[]{:S(2)}) %collective-permute-start.69) | collective-permute-done | bytes 2621472 | tf_op jit(solution)/shard_map/cond/branch_5_fun/ppermute | solution.py:475
  157.8 4.6 %collective-permute-start.71 = (f32[20,2,128,128]{3,2,1,0:T(8,128)S(1)}, f32[20,2,128,128]{3,2,1,0:T(8,128)S(1)}, u32[]{:S(2)}, u32[]{:S(2)}) collective-permute-start(f32[20,2,128,128]{3,2,1,0:T(8,128)S(1)} %collective-permute-done.68.refs_2_.refs_4_), channel_id=1, source_target_pairs={{0,4},{2,6},{4,8},{6,10},{8,12},{10,14},{1,5},{3,7},{5,9},{7,11},{... | collective-permute-start | bytes 7864328 | tf_op jit(solution)/shard_map/cond/branch_5_fun/ppermute | solution.py:475
  163.7 37.8 %gemm_units.67.refs_0_ = f32[4,1536,256]{2,1,0:T(8,128)S(1)} custom-call(s32[474]{0:T(512)S(1)} %get-tuple-element.254.plan, s32[2]{0:T(128)S(1)} %get-tuple-element.255.place, f32[4,1536,256]{2,1,0:T(8,128)S(1)} %gemm_units.66.refs_0_, f32[2,1536,6144]{2,1,0:T(8,128)} %get-tuple-element.259.refs_0_.refs_1_, ...), custom_call_target="tpu_custom_call", output_to_operand_aliasing={{}: (2, {})} | custom-call | flops 21743271936 | bytes 40894464 | tf_op jit(solution)/shard_map/cond/branch_5_fun/gemm_units/pallas_call | solution.py:287
  201.5 10.6 %collective-permute-done.73.refs_4_.refs_9_ = f32[20,2,128,128]{3,2,1,0:T(8,128)S(1)} collective-permute-done((f32[20,2,128,128]{3,2,1,0:T(8,128)S(1)}, f32[20,2,128,128]{3,2,1,0:T(8,128)S(1)}, u32[]{:S(2)}, u32[]{:S(2)}) %collective-permute-start.73) | collective-permute-done | bytes 2621472 | tf_op jit(solution)/shard_map/cond/branch_5_fun/ppermute | solution.py:481
  212.2 3.5 collective-permute-done.71.refs_2_.refs_7_
  215.6 4.3 %collective-permute-done.72.refs_3_.refs_8_ = f32[20,2,128,128]{3,2,1,0:T(8,128)S(1)} collective-permute-done((f32[20,2,128,128]{3,2,1,0:T(8,128)S(1)}, f32[20,2,128,128]{3,2,1,0:T(8,128)S(1)}, u32[]{:S(2)}, u32[]{:S(2)}) %collective-permute-start.72) | collective-permute-done | bytes 2621472 | tf_op jit(solution)/shard_map/cond/branch_5_fun/ppermute | solution.py:475
  225.4 30.9 %gemm_units.68.refs_0_ = f32[4,1536,256]{2,1,0:T(8,128)S(1)} custom-call(s32[474]{0:T(512)S(1)} %get-tuple-element.254.plan, s32[2]{0:T(128)S(1)} %get-tuple-element.255.place, f32[4,1536,256]{2,1,0:T(8,128)S(1)} %gemm_units.67.refs_0_, f32[2,1536,6144]{2,1,0:T(8,128)} %get-tuple-element.259.refs_0_.refs_1_, ...), custom_call_target="tpu_custom_call", output_to_operand_aliasing={{}: (2, {})} | custom-call | flops 21743271936 | bytes 40894464 | tf_op jit(solution)/shard_map/cond/branch_5_fun/gemm_units/pallas_call | solution.py:287
  256.8 16.9 %gemm_units.69.mine = f32[4,1536,256]{2,1,0:T(8,128)S(1)} custom-call(s32[474]{0:T(512)S(1)} %get-tuple-element.254.plan, s32[2]{0:T(128)S(1)} %get-tuple-element.255.place, f32[4,1536,256]{2,1,0:T(8,128)S(1)} %gemm_units.68.refs_0_, f32[2,1536,6144]{2,1,0:T(8,128)} %get-tuple-element.259.refs_0_.refs_1_, ...), custom_call_target="tpu_custom_call", output_to_operand_aliasing={{}: (2, {})} | custom-call | flops 7247757312 | bytes 22020096 | tf_op jit(solution)/shard_map/cond/branch_5_fun/gemm_units/pallas_call | solution.py:287
  273.8 10.1 %collective-permute-done.77.other = f32[4,1536,256]{2,1,0:T(8,128)S(1)} collective-permute-done((f32[4,1536,256]{2,1,0:T(8,128)S(1)}, f32[4,1536,256]{2,1,0:T(8,128)S(1)}, u32[]{:S(2)}, u32[]{:S(2)}) %collective-permute-start.77) | collective-permute-done | bytes 6291488 | tf_op jit(solution)/shard_map/cond/branch_5_fun/ppermute | solution.py:481
  288.4 16.8 %finish_columns.13 = (f32[4,2,1536,128]{3,2,1,0:T(8,128)}, f32[6,2,128,128]{3,2,1,0:T(8,128)}) custom-call(s32[474]{0:T(512)S(1)} %get-tuple-element.254.plan, s32[2]{0:T(128)S(1)} %get-tuple-element.255.place, s32[4]{0:T(128)S(1)} %get-tuple-element.256.order, f32[4,1536,256]{2,1,0:T(8,128)} %copy-done, f32[4,1536,256]{2,1,0:T(8,128)} %copy-done.51, ...), custom_call_target="tpu_custom_call" | custom-call | tf_op jit(solution)/shard_map/cond/branch_5_fun/finish_columns/pallas_call | solution.py:411
  318.9 7.1 %collective-permute-start.105 = (f32[4,96,128]{2,1,0:T(8,128)S(1)}, f32[4,96,128]{2,1,0:T(8,128)S(1)}, u32[]{:S(2)}, u32[]{:S(2)}) collective-permute-start(f32[4,96,128]{2,1,0:T(8,128)S(1)} %dynamic-slice_bitcast_fusion.1), channel_id=1, source_target_pairs={{0,2},{2,0},{4,6},{6,4},{8,10},{10,8},{12,14},{14,12},{1,3},{3,1},... | collective-permute-start | bytes 589832 | tf_op jit(solution)/shard_map/ppermute | solution.py:481
  326.0 5.2 %collective-permute-done.105 = f32[4,96,128]{2,1,0:T(8,128)S(1)} collective-permute-done((f32[4,96,128]{2,1,0:T(8,128)S(1)}, f32[4,96,128]{2,1,0:T(8,128)S(1)}, u32[]{:S(2)}, u32[]{:S(2)}) %collective-permute-start.105) | collective-permute-done | bytes 196640 | tf_op jit(solution)/shard_map/ppermute | solution.py:481
  331.3 6.1 %collective-permute-start.107 = (f32[96,128]{1,0:T(8,128)S(1)}, f32[96,128]{1,0:T(8,128)S(1)}, u32[]{:S(2)}, u32[]{:S(2)}) collective-permute-start(f32[96,128]{1,0:T(8,128)S(1)} %get-tuple-element.372), channel_id=1, source_target_pairs={{0,8},{2,10},{4,12},{6,14},{8,0},{10,2},{12,4},{14,6},{1,9},{3,11}... | collective-permute-start | bytes 147464 | tf_op jit(solution)/shard_map/ppermute | solution.py:500
  349.3 5.2 %collective-permute-done.112 = f32[4,96,128]{2,1,0:T(8,128)S(1)} collective-permute-done((f32[4,96,128]{2,1,0:T(8,128)S(1)}, f32[4,96,128]{2,1,0:T(8,128)S(1)}, u32[]{:S(2)}, u32[]{:S(2)}) %collective-permute-start.112) | collective-permute-done | bytes 196640 | tf_op jit(solution)/shard_map/ppermute | solution.py:481
  (77 shorter events, 48.6 us)
Async XLA Ops:
  23.8 61.3 %collective-permute-start.65 = (f32[20,2,128,128]{3,2,1,0:T(8,128)}, f32[20,2,128,128]{3,2,1,0:T(8,128)S(1)}, u32[]{:S(2)}, u32[]{:S(2)}) collective-permute-start(f32[20,2,128,128]{3,2,1,0:T(8,128)} %slice.63.refs_1_.refs_0_), channel_id=1, source_target_pairs={{0,4},{2,6},{4,8},{6,10},{8,12},{10,14},{1,5},{3,7},{5,9},{7,11},{... | collective-permute-start | bytes 7864328 | tf_op jit(solution)/shard_map/cond/branch_5_fun/ppermute | solution.py:475
  28.9 60.5 %collective-permute-start.66 = (f32[20,2,128,128]{3,2,1,0:T(8,128)}, f32[20,2,128,128]{3,2,1,0:T(8,128)}, u32[]{:S(2)}, u32[]{:S(2)}) collective-permute-start(f32[20,2,128,128]{3,2,1,0:T(8,128)} %slice.63.refs_1_.refs_0_), channel_id=1, source_target_pairs={{4,0},{6,2},{8,4},{10,6},{12,8},{14,10},{5,1},{7,3},{9,5},{11,7},{... | collective-permute-start | bytes 7864328 | tf_op jit(solution)/shard_map/cond/branch_5_fun/ppermute | solution.py:475
  30.3 59.1 %collective-permute-start.67 = (f32[20,2,128,128]{3,2,1,0:T(8,128)}, f32[20,2,128,128]{3,2,1,0:T(8,128)}, u32[]{:S(2)}, u32[]{:S(2)}) collective-permute-start(f32[20,2,128,128]{3,2,1,0:T(8,128)} %slice.63.refs_1_.refs_0_), channel_id=1, source_target_pairs={{0,2},{2,0},{4,6},{6,4},{8,10},{10,8},{12,14},{14,12},{1,3},{3,1},... | collective-permute-start | bytes 7864328 | tf_op jit(solution)/shard_map/cond/branch_5_fun/ppermute | solution.py:481
  93.0 58.5 %collective-permute-start.68 = (f32[20,2,128,128]{3,2,1,0:T(8,128)S(1)}, f32[20,2,128,128]{3,2,1,0:T(8,128)S(1)}, u32[]{:S(2)}, u32[]{:S(2)}) collective-permute-start(f32[20,2,128,128]{3,2,1,0:T(8,128)S(1)} %get-tuple-element.358), channel_id=1, source_target_pairs={{0,4},{2,6},{4,8},{6,10},{8,12},{10,14},{1,5},{3,7},{5,9},{7,11},{... | collective-permute-start | bytes 7864328 | tf_op jit(solution)/shard_map/cond/branch_5_fun/ppermute | solution.py:475
  97.1 58.7 %collective-permute-start.69 = (f32[20,2,128,128]{3,2,1,0:T(8,128)S(1)}, f32[20,2,128,128]{3,2,1,0:T(8,128)S(1)}, u32[]{:S(2)}, u32[]{:S(2)}) collective-permute-start(f32[20,2,128,128]{3,2,1,0:T(8,128)S(1)} %get-tuple-element.359), channel_id=1, source_target_pairs={{4,0},{6,2},{8,4},{10,6},{12,8},{14,10},{5,1},{7,3},{9,5},{11,7},{... | collective-permute-start | bytes 7864328 | tf_op jit(solution)/shard_map/cond/branch_5_fun/ppermute | solution.py:475
  98.4 57.4 %collective-permute-start.70 = (f32[20,2,128,128]{3,2,1,0:T(8,128)S(1)}, f32[20,2,128,128]{3,2,1,0:T(8,128)S(1)}, u32[]{:S(2)}, u32[]{:S(2)}) collective-permute-start(f32[20,2,128,128]{3,2,1,0:T(8,128)S(1)} %get-tuple-element.357), channel_id=1, source_target_pairs={{0,2},{2,0},{4,6},{6,4},{8,10},{10,8},{12,14},{14,12},{1,3},{3,1},... | collective-permute-start | bytes 7864328 | tf_op jit(solution)/shard_map/cond/branch_5_fun/ppermute | solution.py:481
  156.2 56.0 %collective-permute-start.73 = (f32[20,2,128,128]{3,2,1,0:T(8,128)S(1)}, f32[20,2,128,128]{3,2,1,0:T(8,128)S(1)}, u32[]{:S(2)}, u32[]{:S(2)}) collective-permute-start(f32[20,2,128,128]{3,2,1,0:T(8,128)S(1)} %broadcast_select_fusion.25), channel_id=1, source_target_pairs={{0,2},{2,0},{4,6},{6,4},{8,10},{10,8},{12,14},{14,12},{1,3},{3,1},... | collective-permute-start | bytes 7864328 | tf_op jit(solution)/shard_map/cond/branch_5_fun/ppermute | solution.py:481
  157.8 57.9 %collective-permute-start.71 = (f32[20,2,128,128]{3,2,1,0:T(8,128)S(1)}, f32[20,2,128,128]{3,2,1,0:T(8,128)S(1)}, u32[]{:S(2)}, u32[]{:S(2)}) collective-permute-start(f32[20,2,128,128]{3,2,1,0:T(8,128)S(1)} %collective-permute-done.68.refs_2_.refs_4_), channel_id=1, source_target_pairs={{0,4},{2,6},{4,8},{6,10},{8,12},{10,14},{1,5},{3,7},{5,9},{7,11},{... | collective-permute-start | bytes 7864328 | tf_op jit(solution)/shard_map/cond/branch_5_fun/ppermute | solution.py:475
  162.4 57.5 %collective-permute-start.72 = (f32[20,2,128,128]{3,2,1,0:T(8,128)S(1)}, f32[20,2,128,128]{3,2,1,0:T(8,128)S(1)}, u32[]{:S(2)}, u32[]{:S(2)}) collective-permute-start(f32[20,2,128,128]{3,2,1,0:T(8,128)S(1)} %collective-permute-done.69.refs_3_.refs_5_), channel_id=1, source_target_pairs={{4,0},{6,2},{8,4},{10,6},{12,8},{14,10},{5,1},{7,3},{9,5},{11,7},{... | collective-permute-start | bytes 7864328 | tf_op jit(solution)/shard_map/cond/branch_5_fun/ppermute | solution.py:475
  220.0 36.3 %collective-permute-start.74 = (f32[10,2,128,128]{3,2,1,0:T(8,128)S(1)}, f32[10,2,128,128]{3,2,1,0:T(8,128)S(1)}, u32[]{:S(2)}, u32[]{:S(2)}) collective-permute-start(f32[10,2,128,128]{3,2,1,0:T(8,128)S(1)} %slice.64), channel_id=1, source_target_pairs={{0,4},{2,6},{4,8},{6,10},{8,12},{10,14},{1,5},{3,7},{5,9},{7,11},{... | collective-permute-start | bytes 3932168 | tf_op jit(solution)/shard_map/cond/branch_5_fun/ppermute | solution.py:475
  223.4 33.0 %collective-permute-start.75 = (f32[10,2,128,128]{3,2,1,0:T(8,128)S(1)}, f32[10,2,128,128]{3,2,1,0:T(8,128)S(1)}, u32[]{:S(2)}, u32[]{:S(2)}) collective-permute-start(f32[10,2,128,128]{3,2,1,0:T(8,128)S(1)} %slice.64), channel_id=1, source_target_pairs={{4,0},{6,2},{8,4},{10,6},{12,8},{14,10},{5,1},{7,3},{9,5},{11,7},{... | collective-permute-start | bytes 3932168 | tf_op jit(solution)/shard_map/cond/branch_5_fun/ppermute | solution.py:475
  224.8 31.5 %collective-permute-start.76 = (f32[10,2,128,128]{3,2,1,0:T(8,128)S(1)}, f32[10,2,128,128]{3,2,1,0:T(8,128)S(1)}, u32[]{:S(2)}, u32[]{:S(2)}) collective-permute-start(f32[10,2,128,128]{3,2,1,0:T(8,128)S(1)} %slice_select_fusion.5), channel_id=1, source_target_pairs={{0,2},{2,0},{4,6},{6,4},{8,10},{10,8},{12,14},{14,12},{1,3},{3,1},... | collective-permute-start | bytes 3932168 | tf_op jit(solution)/shard_map/cond/branch_5_fun/ppermute | solution.py:481
  256.8 29.8 %copy-start.27 = (f32[20,2,128,128]{3,2,1,0:T(8,128)S(1)}, f32[20,2,128,128]{3,2,1,0:T(8,128)}, u32[]{:S(2)}) copy-start(f32[20,2,128,128]{3,2,1,0:T(8,128)} %copy-done.26) | copy-start | bytes 7864324 | tf_op jit(solution)/shard_map/cond
  273.7 10.2 %collective-permute-start.77 = (f32[4,1536,256]{2,1,0:T(8,128)S(1)}, f32[4,1536,256]{2,1,0:T(8,128)S(1)}, u32[]{:S(2)}, u32[]{:S(2)}) collective-permute-start(f32[4,1536,256]{2,1,0:T(8,128)S(1)} %gemm_units.69.mine), channel_id=1, source_target_pairs={{0,1},{1,0},{2,3},{3,2},{4,5},{5,4},{6,7},{7,6},{8,9},{9,8},{10,11... | collective-permute-start | bytes 18874376 | tf_op jit(solution)/shard_map/cond/branch_5_fun/ppermute | solution.py:481
  316.0 1.8 collective-permute-start.104
  318.9 12.3 %collective-permute-start.105 = (f32[4,96,128]{2,1,0:T(8,128)S(1)}, f32[4,96,128]{2,1,0:T(8,128)S(1)}, u32[]{:S(2)}, u32[]{:S(2)}) collective-permute-start(f32[4,96,128]{2,1,0:T(8,128)S(1)} %dynamic-slice_bitcast_fusion.1), channel_id=1, source_target_pairs={{0,2},{2,0},{4,6},{6,4},{8,10},{10,8},{12,14},{14,12},{1,3},{3,1},... | collective-permute-start | bytes 589832 | tf_op jit(solution)/shard_map/ppermute | solution.py:481
  331.2 7.8 %collective-permute-start.106 = (f32[96,128]{1,0:T(8,128)S(1)}, f32[96,128]{1,0:T(8,128)S(1)}, u32[]{:S(2)}, u32[]{:S(2)}) collective-permute-start(f32[96,128]{1,0:T(8,128)S(1)} %get-tuple-element.370), channel_id=1, source_target_pairs={{0,4},{2,6},{4,8},{6,10},{8,12},{10,14},{12,0},{14,2},{1,5},{3,7},... | collective-permute-start | bytes 147464 | tf_op jit(solution)/shard_map/ppermute | solution.py:500
  331.3 9.3 %collective-permute-start.107 = (f32[96,128]{1,0:T(8,128)S(1)}, f32[96,128]{1,0:T(8,128)S(1)}, u32[]{:S(2)}, u32[]{:S(2)}) collective-permute-start(f32[96,128]{1,0:T(8,128)S(1)} %get-tuple-element.372), channel_id=1, source_target_pairs={{0,8},{2,10},{4,12},{6,14},{8,0},{10,2},{12,4},{14,6},{1,9},{3,11}... | collective-permute-start | bytes 147464 | tf_op jit(solution)/shard_map/ppermute | solution.py:500
  337.4 4.1 %collective-permute-start.108 = (f32[96,128]{1,0:T(8,128)S(1)}, f32[96,128]{1,0:T(8,128)S(1)}, u32[]{:S(2)}, u32[]{:S(2)}) collective-permute-start(f32[96,128]{1,0:T(8,128)S(1)} %get-tuple-element.371), channel_id=1, source_target_pairs={{0,12},{2,14},{4,0},{6,2},{8,4},{10,6},{12,8},{14,10},{1,13},{3,15... | collective-permute-start | bytes 147464 | tf_op jit(solution)/shard_map/ppermute | solution.py:500
  341.5 6.0 %collective-permute-start.109 = (f32[96,128]{1,0:T(8,128)S(1)}, f32[96,128]{1,0:T(8,128)S(1)}, u32[]{:S(2)}, u32[]{:S(2)}) collective-permute-start(f32[96,128]{1,0:T(8,128)S(1)} %get-tuple-element.341), channel_id=1, source_target_pairs={{0,4},{2,6},{4,8},{6,10},{8,12},{10,14},{12,0},{14,2},{1,5},{3,7},... | collective-permute-start | bytes 147464 | tf_op jit(solution)/shard_map/ppermute | solution.py:500
  342.1 6.5 %collective-permute-start.110 = (f32[96,128]{1,0:T(8,128)S(1)}, f32[96,128]{1,0:T(8,128)S(1)}, u32[]{:S(2)}, u32[]{:S(2)}) collective-permute-start(f32[96,128]{1,0:T(8,128)S(1)} %get-tuple-element.341), channel_id=1, source_target_pairs={{0,8},{2,10},{4,12},{6,14},{8,0},{10,2},{12,4},{14,6},{1,9},{3,11}... | collective-permute-start | bytes 147464 | tf_op jit(solution)/shard_map/ppermute | solution.py:500
  344.4 4.4 %collective-permute-start.111 = (f32[96,128]{1,0:T(8,128)S(1)}, f32[96,128]{1,0:T(8,128)S(1)}, u32[]{:S(2)}, u32[]{:S(2)}) collective-permute-start(f32[96,128]{1,0:T(8,128)S(1)} %get-tuple-element.341), channel_id=1, source_target_pairs={{0,12},{2,14},{4,0},{6,2},{8,4},{10,6},{12,8},{14,10},{1,13},{3,15... | collective-permute-start | bytes 147464 | tf_op jit(solution)/shard_map/ppermute | solution.py:500
  348.8 5.7 %collective-permute-start.112 = (f32[4,96,128]{2,1,0:T(8,128)S(1)}, f32[4,96,128]{2,1,0:T(8,128)S(1)}, u32[]{:S(2)}, u32[]{:S(2)}) collective-permute-start(f32[4,96,128]{2,1,0:T(8,128)S(1)} %bitcast_dynamic-update-slice_fusion), channel_id=1, source_target_pairs={{0,2},{2,0},{4,6},{6,4},{8,10},{10,8},{12,14},{14,12},{1,3},{3,1},... | collective-permute-start | bytes 589832 | tf_op jit(solution)/shard_map/ppermute | solution.py:481
  354.6 1.8 collective-permute-start.113
  (10 other events, 86.3 us)
